TPU v7x, 512 devices: a whole 4x4x16 slice. The times are simulated.
512 devices in a mesh: axial: 16 (over y_lo, x, core), circ: 32 (over z, y_hi).
Axes of the slice: x: 4, y: 4 (y_hi: 2, y_lo: 2; y = y_hi * 2 + y_lo), z: 16, core: 2. Of those that a mesh axis runs over, the one named last changes fastest.
Arguments:
- lam_h: bfloat16 [32, 64, 128, 512], P('axial', 'circ'), may hold values from -6 to 6
- lam_v: bfloat16 [32, 64, 128, 512], P('axial', 'circ'), may hold values from -6 to 6
- panel: bfloat16 [32, 64, 512, 512], P('axial', 'circ')
- corner_panel: bfloat16 [32, 64, 512, 128], P('axial', 'circ'), may hold values from -0.25 to 0.25
- coarse_diag: float32 [32, 128, 128], P('axial'), may hold values from -0.0625 to 0.0625
- coarse_link: float32 [32, 128, 128], P('axial')
- edge_slot: int32 [32, 64, 4], P('axial', 'circ'), may hold values from 0 to 3, as said below
Outputs:
- jump_h: bfloat16 [32, 64, 128, 512], P('axial', 'circ')
- jump_v: bfloat16 [32, 64, 128, 512], P('axial', 'circ')
Inputs may be any that keep to these rules, and one draw needn't show every extreme that they name: For each subdomain (a, c) the four entries edge_slot[a, c, 0], ..., edge_slot[a, c, 3] are 0, 1, 2, 3 in some order, drawn independently for each subdomain; within a subdomain row each value occurs 64 times.
All inputs are finite; a program needn't handle non-finite values.
Results may differ from a plain program's by a relative error of at most 0.0061.
Values may be sent and summed in bfloat16 or wider, within the bound.
No kernel may reach another device: no remote copies, remote signals or barrier semaphores. Data moves between devices by JAX's collectives and lax.ppermute only.
A program may use at most 64 MiB of HBM per device.

v0:
```python
import jax
import jax.numpy as jnp
from jax import lax
from jax.sharding import PartitionSpec as P

E = 128
P_SIZE = 512
NCOR = 128
SA = 2
SC = 2
R = 512


def prefix(array, axis, combine, identity):
    count, position = (lax.axis_size(axis), lax.axis_index(axis))
    everything = jax.tree.map(lambda part: lax.all_gather(part, axis), array)
    start = jax.tree.map(
        lambda part, zero: jnp.broadcast_to(jnp.asarray(zero, part.dtype), part.shape),
        array,
        identity,
    )

    def hop(k, before):
        at = count - 1 - k
        reached = at > position
        new = combine(before, jax.tree.map(lambda part: part[at], everything))
        return jax.tree.map(lambda a, b: jnp.where(reached, a, b), new, before)

    return lax.fori_loop(0, count, hop, start)


def passed_along(array, axis, by):
    count = lax.axis_size(axis)
    return lax.ppermute(array, axis, [(i, (i + by) % count) for i in range(count)])


def passed_along_2(value, axis, steps):
    count = lax.axis_size(axis)
    first, last = (max(0, -steps), min(count, count - steps))
    return lax.ppermute(value, axis, [(source, source + steps) for source in range(first, last)])


def sweep_rows(totals, coarse_diag, coarse_link):
    highest = lax.Precision.HIGHEST
    columns = totals.shape[2]
    identity = jnp.eye(NCOR, dtype=jnp.float32)
    matrix = identity
    vector = jnp.zeros((NCOR, columns), jnp.float32)
    for row in reversed(range(SA)):
        vector = jnp.dot(coarse_diag[row], totals[row], precision=highest) + jnp.dot(
            coarse_link[row], vector, precision=highest
        )
        matrix = jnp.dot(coarse_link[row], matrix, precision=highest)

    def combine(earlier, later):
        return (
            jnp.dot(later[0], earlier[0], precision=highest),
            jnp.dot(later[0], earlier[1], precision=highest) + later[1],
        )

    above = prefix(
        (matrix, vector), "axial", combine, (identity, jnp.zeros((NCOR, columns), jnp.float32))
    )
    carry = above[1]
    results = []
    for row in reversed(range(SA)):
        carry = jnp.dot(coarse_diag[row], totals[row], precision=highest) + jnp.dot(
            coarse_link[row], carry, precision=highest
        )
        results.append(carry)
    return jnp.stack(results[::-1], axis=0)


def on_device(lam_h, lam_v, panel, corner_panel, coarse_diag, coarse_link, edge_slot):
    from_left = passed_along(lam_h[:, SC - 1], "circ", 1)
    lower_h = jnp.concatenate([from_left[:, None], lam_h[:, : SC - 1]], axis=1)
    from_below = passed_along_2(lam_v[SA - 1], "axial", 1)
    lower_v = jnp.concatenate([from_below[None], lam_v[: SA - 1]], axis=0)
    edges = jnp.stack([lam_h, -lower_h, lam_v, -lower_v], axis=2)
    slots = (edge_slot[..., None] == jnp.arange(4, dtype=jnp.int32)).astype(jnp.bfloat16)
    placed = jnp.einsum("abkj,abker->abjer", slots, edges, preferred_element_type=jnp.float32)
    placed = placed.astype(jnp.bfloat16).reshape(SA, SC, P_SIZE, R)
    flexed = jnp.einsum("abpq,abpr->abqr", panel, placed, preferred_element_type=jnp.float32)
    flexed_round = flexed.astype(jnp.bfloat16)
    partial_sums = jnp.einsum(
        "abpk,abpr->akr", corner_panel, flexed_round, preferred_element_type=jnp.float32
    )
    totals = lax.psum(partial_sums, "circ")
    correction = sweep_rows(totals, coarse_diag, coarse_link).astype(jnp.bfloat16)
    update = flexed - jnp.einsum(
        "abpk,akr->abpr", corner_panel, correction, preferred_element_type=jnp.float32
    )
    update = update.astype(jnp.bfloat16).reshape(SA, SC, 4, E, R)
    picked = jnp.einsum(
        "abkj,abjer->abker", slots, update, preferred_element_type=jnp.float32
    ).astype(jnp.bfloat16)
    left_blocks = picked[:, :, 1]
    down_blocks = picked[:, :, 3]
    from_right = passed_along(left_blocks[:, 0], "circ", -1)
    next_left = jnp.concatenate([left_blocks[:, 1:], from_right[:, None]], axis=1)
    from_above = passed_along_2(down_blocks[0], "axial", -1)
    next_down = jnp.concatenate([down_blocks[1:], from_above[None]], axis=0)
    jump_h = (picked[:, :, 0].astype(jnp.float32) - next_left.astype(jnp.float32)).astype(
        jnp.bfloat16
    )
    jump_v = (picked[:, :, 2].astype(jnp.float32) - next_down.astype(jnp.float32)).astype(
        jnp.bfloat16
    )
    return (jump_h, jump_v)


def solution(mesh):
    return jax.shard_map(
        on_device,
        mesh=mesh,
        in_specs=(
            P("axial", "circ", None, None),
            P("axial", "circ", None, None),
            P("axial", "circ", None, None),
            P("axial", "circ", None, None),
            P("axial", None, None),
            P("axial", None, None),
            P("axial", "circ", None),
        ),
        out_specs=(P("axial", "circ", None, None), P("axial", "circ", None, None)),
        check_vma=False,
    )
```

profile of v0, /device:TPU:6, one launch (start us, length us, event | category | flops | bytes accessed | tf_op | source)
XLA Modules:
  0.0 464.0 jit_solution(4723902567054581945)
XLA Ops:
  9.3 5.2 %collective-permute-start = (bf16[2,128,512]{2,1,0:T(8,128)(2,1)S(1)}, bf16[2,128,512]{2,1,0:T(8,128)(2,1)S(1)}, u32[]{:S(2)}, u32[]{:S(2)}) collective-permute-start(bf16[2,128,512]{2,1,0:T(8,128)(2,1)S(1)} %get-tuple-element.187), channel_id=1, source_target_pairs={{0,1},{1,2},{2,3},{3,4},{4,5},{5,6},{6,7},{7,8},{8,9},{9,10},{10,1... | collective-permute-start | bytes 786440 | tf_op jit(solution)/shard_map/ppermute | solution.py:34
  15.7 1.9 collective-permute-start.1
  20.1 9.7 %collective-permute-done = bf16[2,128,512]{2,1,0:T(8,128)(2,1)S(1)} collective-permute-done((bf16[2,128,512]{2,1,0:T(8,128)(2,1)S(1)}, bf16[2,128,512]{2,1,0:T(8,128)(2,1)S(1)}, u32[]{:S(2)}, u32[]{:S(2)}) %collective-permute-start) | collective-permute-done | bytes 262176 | tf_op jit(solution)/shard_map/ppermute | solution.py:34
  30.7 3.8 maximum_negate_fusion
  34.5 5.8 %fusion.20 = bf16[2,2,4,128,512]{4,2,3,1,0:T(4,128)(2,1)S(1)} fusion(bf16[2,2,1,128,512]{4,2,3,1,0:T(2,128)(2,1)S(1)} %get-tuple-element.192, bf16[2,2,1,128,512]{4,2,3,1,0:T(2,128)(2,1)S(1)} %copy.48, bf16[2,2,1,128,512]{4,2,3,1,0:T(2,128)(2,1)S(1)} %get-tuple-element.191, bf16[2,2,1,128,512]{4,2,3,1,0:T(2,128)(2,1)S(1)} %copy.47, s32[2,2,4]{2,1,0:T(2,128)S(1)} %copy-done.7), kind=kOutput, calls=%fused_computation.23 | convolution fusion | flops 17825856 | bytes 4194368 | tf_op jit(solution)/shard_map/abkj,abker->abjer/dot_general | solution.py:81
  42.1 1.9 copy-done.1
  44.0 1.7 fusion.26
  47.3 302.9 %all-reduce.2.cloned.1.call-done = f32[2,128,512]{1,2,0:T(8,128)} async-done(((f32[2,128,512]{1,2,0:T(8,128)}), f32[2,128,512]{1,2,0:T(8,128)}) %all-reduce.2.cloned.1.call-update) | async-done | bytes 524304 | tf_op jit(solution)/shard_map/psum | solution.py:88
  354.1 2.6 copy.66
  356.7 45.4 %all-gather.7.cloned.1.call-done = f32[2048,512]{0,1:T(8,128)} async-done(((f32[128,512]{0,1:T(8,128)}), f32[2048,512]{0,1:T(8,128)}) %all-gather.7.cloned.1.call-update) | async-done | bytes 4194320 | tf_op jit(solution)/shard_map/all_gather | solution.py:16
  402.1 5.4 %copy.67 = f32[2048,512]{1,0:T(8,128)} copy(f32[2048,512]{0,1:T(8,128)} %all-gather.7.cloned.1.call-done) | data formatting | bytes 8388608
  407.5 22.9 %while.16 = (s32[]{:T(128)}, f32[128,512]{1,0:T(8,128)S(1)}, s32[]{:T(128)}, f32[16,128,128]{2,1,0:T(8,128)}, f32[16,128,512]{2,1,0:T(8,128)}, /*index=5*/s32[]{:T(128)}, s32[]{:T(128)}, s32[]{:T(128)}, s32[]{:T(128)}) while((s32[]{:T(128)}, f32[128,512]{1,0:T(8,128)S(1)}, s32[]{:T(128)}, f32[16,128,128]{2,1,0:T(8,128)}, ...), condition=%wide.region_3.4_spmd.clone, body=%wide.region_2.3_spmd.clone.sunk | while | flops 100925448 | bytes 1641117 | solution.py:29
  407.5 1.4 fusion.83
  409.0 1.4 fusion.83
  410.4 1.4 fusion.83
  411.8 1.4 fusion.83
  413.3 1.4 fusion.83
  414.7 1.4 fusion.83
  416.1 1.4 fusion.83
  417.6 1.4 fusion.83
  419.0 1.4 fusion.83
  420.4 1.4 fusion.83
  421.9 1.4 fusion.83
  423.3 1.4 fusion.83
  427.6 1.4 fusion.83
  429.0 1.4 fusion.83
  431.4 2.9 fusion.8
  434.4 1.8 fusion.23
  437.3 3.4 collective-permute-start.3
  440.7 2.2 slice_convert_fusion
  443.2 6.7 %collective-permute-start.2 = (bf16[2,128,512]{2,1,0:T(8,128)(2,1)S(1)}, bf16[2,128,512]{2,1,0:T(8,128)(2,1)S(1)}, u32[]{:S(2)}, u32[]{:S(2)}) collective-permute-start(bf16[2,128,512]{2,1,0:T(8,128)(2,1)S(1)} %get-tuple-element.186), channel_id=1, source_target_pairs={{0,31},{1,0},{2,1},{3,2},{4,3},{5,4},{6,5},{7,6},{8,7},{9,8},{10,9... | collective-permute-start | bytes 786440 | tf_op jit(solution)/shard_map/ppermute | solution.py:34
  450.9 4.6 collective-permute-done.2
  (69 shorter events, 20.1 us)
Async XLA Ops:
  8.0 32.8 %copy-start = (bf16[2,2,512,512]{3,2,1,0:T(8,128)(2,1)S(1)}, bf16[2,2,512,512]{3,2,1,0:T(8,128)(2,1)}, u32[]{:S(2)}) copy-start(bf16[2,2,512,512]{3,2,1,0:T(8,128)(2,1)} %param.11) | copy-start | bytes 6291460
  8.0 10.4 %copy-start.3 = (bf16[2,2,128,512]{3,2,1,0:T(8,128)(2,1)S(1)}, bf16[2,2,128,512]{3,2,1,0:T(8,128)(2,1)}, u32[]{:S(2)}) copy-start(bf16[2,2,128,512]{3,2,1,0:T(8,128)(2,1)} %param.9) | copy-start | bytes 1572868
  8.0 342.3 %all-reduce.2.cloned.1.call-start = ((), (), s32[]{:S(2)}) async-start(), calls=%async_computation | async-start | bytes 1048576 | tf_op jit(solution)/shard_map/psum | solution.py:88
  9.3 9.9 %copy-start.4 = (bf16[2,2,128,512]{3,2,1,0:T(8,128)(2,1)S(1)}, bf16[2,2,128,512]{3,2,1,0:T(8,128)(2,1)}, u32[]{:S(2)}) copy-start(bf16[2,2,128,512]{3,2,1,0:T(8,128)(2,1)} %param.10) | copy-start | bytes 1572868
  9.3 20.5 %collective-permute-start = (bf16[2,128,512]{2,1,0:T(8,128)(2,1)S(1)}, bf16[2,128,512]{2,1,0:T(8,128)(2,1)S(1)}, u32[]{:S(2)}, u32[]{:S(2)}) collective-permute-start(bf16[2,128,512]{2,1,0:T(8,128)(2,1)S(1)} %get-tuple-element.187), channel_id=1, source_target_pairs={{0,1},{1,2},{2,3},{3,4},{4,5},{5,6},{6,7},{7,8},{8,9},{9,10},{10,1... | collective-permute-start | bytes 786440 | tf_op jit(solution)/shard_map/ppermute | solution.py:34
  15.7 14.6 %collective-permute-start.1 = (bf16[2,128,512]{2,1,0:T(8,128)(2,1)S(1)}, bf16[2,128,512]{2,1,0:T(8,128)(2,1)S(1)}, u32[]{:S(2)}, u32[]{:S(2)}) collective-permute-start(bf16[2,128,512]{2,1,0:T(8,128)(2,1)S(1)} %get-tuple-element.189), channel_id=1, source_target_pairs={{0,32},{32,64},{64,96},{96,128},{128,160},{160,192},{192,224},{224... | collective-permute-start | bytes 786440 | tf_op jit(solution)/shard_map/ppermute | solution.py:40
  30.6 3.8 copy-start.7
  40.8 3.3 copy-start.2
  42.1 1.9 copy-start.1
  44.0 1.8 copy-start.5
  44.0 306.3 %copy-start.6 = (f32[2,128,128]{2,1,0:T(8,128)S(1)}, f32[2,128,128]{2,1,0:T(8,128)}, u32[]{:S(2)}) copy-start(f32[2,128,128]{2,1,0:T(8,128)} %param.13) | copy-start | bytes 393220
  45.8 308.3 %all-gather.5.cloned.1.call-start = ((), (), s32[]{:S(2)}) async-start(), calls=%async_computation.1 | async-start | bytes 1114112 | tf_op jit(solution)/shard_map/all_gather | solution.py:16
  47.0 355.1 %all-gather.7.cloned.1.call-start = ((), (), s32[]{:S(2)}) async-start(), calls=%async_computation.2 | async-start | bytes 4456448 | tf_op jit(solution)/shard_map/all_gather | solution.py:16
  437.3 12.6 %collective-permute-start.3 = (bf16[2,128,512]{2,1,0:T(8,128)(2,1)S(1)}, bf16[2,128,512]{2,1,0:T(8,128)(2,1)S(1)}, u32[]{:S(2)}, u32[]{:S(2)}) collective-permute-start(bf16[2,128,512]{2,1,0:T(8,128)(2,1)S(1)} %bitcast.145), channel_id=1, source_target_pairs={{32,0},{64,32},{96,64},{128,96},{160,128},{192,160},{224,192},{256... | collective-permute-start | bytes 786440 | tf_op jit(solution)/shard_map/ppermute | solution.py:40
  443.2 12.3 %collective-permute-start.2 = (bf16[2,128,512]{2,1,0:T(8,128)(2,1)S(1)}, bf16[2,128,512]{2,1,0:T(8,128)(2,1)S(1)}, u32[]{:S(2)}, u32[]{:S(2)}) collective-permute-start(bf16[2,128,512]{2,1,0:T(8,128)(2,1)S(1)} %get-tuple-element.186), channel_id=1, source_target_pairs={{0,31},{1,0},{2,1},{3,2},{4,3},{5,4},{6,5},{7,6},{8,7},{9,8},{10,9... | collective-permute-start | bytes 786440 | tf_op jit(solution)/shard_map/ppermute | solution.py:34
Sparse Core Ops, SparseCore 0:
  45.9 304.3 all-reduce.1
Sparse Core Ops, SparseCore 1:
  49.1 37.1 all-gather.4
  354.1 47.9 all-gather.6
where the time goes:
time: 467 us; the launch traced here: 464 us
  waiting for transfers between devices  363 us (78%)
  matrix products  41.3 us (9%)
  local copies, waits for them, and re-layouts  17.7 us (4%)
  starting transfers between devices  17.6 us (4%)
  between operations  15.9 us (3%)
  other arithmetic  8.13 us (2%)
    psum x1, waiting for transfers between devices, on_device(): totals = lax.psum(partial_sums, 'circ')  303 us
    all_gather x2, waiting for transfers between devices, prefix(): everything = jax.tree.map(lambda part: lax.all_gather(part, axis), array)  45.4 us
    dot_general x16, matrix products, combine(): jnp.dot(later[0], earlier[1], precision=highest) + later[1]  21.9 us
    ppermute x2, waiting for transfers between devices, passed_along(): lax.ppermute(array, axis, [(i, (i + by) % count) for i in range(count)])  14.3 us
    ppermute x2, starting transfers between devices, passed_along(): lax.ppermute(array, axis, [(i, (i + by) % count) for i in range(count)])  12 us
    unnamed x21, local copies, waits for them, and re-layouts  10.2 us
  transfers between devices with their start and end apart: 7, of which 4 were waited for; matrix products, arithmetic and copies ran while one was open for 3% of the time, Pallas kernels for 0%

commit v1 on v0

v1 whole, which is shorter than its diff:
```python
import jax
import jax.numpy as jnp
from jax import lax
from jax.experimental import pallas as pl
from jax.experimental.pallas import tpu as pltpu
from jax.sharding import Mesh, PartitionSpec as P

E = 128
P_SIZE = 512
NCOR = 128
R = 512
SPLIT = (2, 4, 2, 16, 2)
AXIAL = ("ylo", "x", "core")
CIRC = ("z", "yhi")
CHIPS = ("ylo", "x")
PLANE = ("ylo", "x", "core", "yhi")
F32 = jnp.float32
BF16 = jnp.bfloat16
HIGHEST = lax.Precision.HIGHEST


def dot(a, b, ca=1, cb=0, precision=None):
    return lax.dot_general(
        a, b, (((ca,), (cb,)), ((), ())), preferred_element_type=F32, precision=precision
    )


def split2(value):
    high = value.astype(BF16)
    return high, (value - high.astype(F32)).astype(BF16)


def dot_nt3(a, b_high, b_low):
    a_high, a_low = split2(a)
    return dot(a_high, b_high, 1, 1) + dot(a_high, b_low, 1, 1) + dot(a_low, b_high, 1, 1)


def rows(slot, a, c, k):
    return pl.ds(pl.multiple_of(slot[a, c, k] * E, E), E)


def prep_kernel(slot, panel, corner, lam_h, lam_v, part, w1, w3):
    w = {}
    for a in range(2):
        for c in range(2):
            for k in range(4):
                w[a, c, k] = dot(panel[a, c, rows(slot, a, c, k), :], corner[a, c])
    for i in range(2):
        w1[i] = w[i, 0, 1].astype(BF16)
        w3[i] = w[0, i, 3].astype(BF16)
    wh = [
        jnp.concatenate([w[a, 0, 0] - w[a, 1, 1], w[a, 1, 0]], axis=0).astype(BF16)
        for a in range(2)
    ]
    wv = [jnp.concatenate([w[a, 0, 2], w[a, 1, 2]], axis=0).astype(BF16) for a in range(2)]
    wl = jnp.concatenate([w[1, 0, 3], w[1, 1, 3]], axis=0).astype(BF16)
    part[:, :NCOR] = dot(lam_h[0], wh[0], 0, 0) + dot(lam_v[0], wv[0], 0, 0)
    part[:, NCOR:] = (
        dot(lam_h[1], wh[1], 0, 0) + dot(lam_v[1], wv[1], 0, 0) - dot(lam_v[0], wl, 0, 0)
    )


def halo_kernel(part, w1, w3, left, below, out):
    out[:, :NCOR] = (
        part[:, :NCOR]
        - dot(left[0], w1[0], 0, 0)
        - dot(below[0], w3[0], 0, 0)
        - dot(below[1], w3[1], 0, 0)
    ).astype(BF16)
    out[:, NCOR:] = (part[:, NCOR:] - dot(left[1], w1[1], 0, 0)).astype(BF16)


def flex_kernel(
    slot, panel, corner, lam_h, lam_v, left, below, base_h, base_v, send_h, send_v, placed, flexed
):
    for a in range(2):
        for c in range(2):
            edges = (
                lam_h[a, c],
                -(lam_h[a, 0] if c else left[a]),
                lam_v[a, c],
                -(lam_v[0, c] if a else below[c]),
            )
            for k in range(4):
                placed[rows(slot, a, c, k), :] = edges[k]
            flexed[...] = dot(panel[a, c], placed[...], 0, 0)
            base_h[a, c] = flexed[rows(slot, a, c, 0), :]
            base_v[a, c] = flexed[rows(slot, a, c, 2), :]
            left_block = flexed[rows(slot, a, c, 1), :]
            down_block = flexed[rows(slot, a, c, 3), :]
            if c:
                base_h[a, 0] = base_h[a, 0] - left_block
            else:
                send_h[a, :, :R] = left_block.astype(BF16)
                send_h[a, :, R:] = corner[a, c, rows(slot, a, c, 1), :]
            if a:
                base_v[0, c] = base_v[0, c] - down_block
            else:
                send_v[c, :, :R] = down_block.astype(BF16)
                send_v[c, :, R:] = corner[a, c, rows(slot, a, c, 3), :]


def pair_kernel(link, pair):
    pair[...] = dot(link[0], link[1], precision=HIGHEST)


def chip_kernel(is_core_1, diag, link, pair, other, chip, terms):
    core_1 = is_core_1[0] == 1
    first = jnp.where(core_1, other[...], pair[...])
    second = jnp.where(core_1, pair[...], other[...])
    value = dot(first, second, precision=HIGHEST)
    for m in range(chip.shape[0]):
        chip[m] = value
    lower = dot(link[0], diag[1], precision=HIGHEST)
    seen_0 = jnp.where(core_1, dot(other[...], diag[0], precision=HIGHEST), diag[0])
    seen_1 = jnp.where(core_1, dot(other[...], lower, precision=HIGHEST), lower)
    table = (
        (seen_0, seen_1),
        (diag[0], lower),
        (jnp.zeros_like(lower), diag[1]),
    )
    for i in range(3):
        for j in range(2):
            high, low = split2(table[i][j])
            place = (slice(i * NCOR, (i + 1) * NCOR), slice(j * NCOR, (j + 1) * NCOR))
            terms[(0, *place)] = high
            terms[(1, *place)] = low


def chain_kernel(where, other, pair, link, chips, chain, own):
    count = chips.shape[0]
    me, core_1 = where[0], where[1] == 1
    eye = (
        lax.broadcasted_iota(jnp.int32, (NCOR, NCOR), 0)
        == lax.broadcasted_iota(jnp.int32, (NCOR, NCOR), 1)
    ).astype(F32)
    value = jnp.where(core_1, eye, other[...])
    for j in range(1, count):
        if j > 1:
            value = dot(value, chips[jnp.minimum(me + j - 1, count - 1)], precision=HIGHEST)
        high, low = split2(jnp.where(me + j < count, value, 0.0))
        chain[0, :, (j - 1) * NCOR : j * NCOR] = high
        chain[1, :, (j - 1) * NCOR : j * NCOR] = low
    for i, matrix in enumerate((pair[...], link[1])):
        high, low = split2(matrix)
        own[0, i * NCOR : (i + 1) * NCOR, :] = high
        own[1, i * NCOR : (i + 1) * NCOR, :] = low


def sum_kernel(where, received, terms, out):
    total = received[0].astype(F32)
    for i in range(1, received.shape[0]):
        total = total + received[i].astype(F32)
    value = dot_nt3(total, terms[0], terms[1])
    seen = value[:, :NCOR].astype(BF16)
    mine = value[:, NCOR : 2 * NCOR].astype(BF16)
    upper = value[:, 2 * NCOR :].astype(BF16)
    for p in range(out.shape[0]):
        out[p, :, :NCOR] = jnp.where(where[0] == p // 4, mine, seen)
        out[p, :, NCOR:] = upper


def carry_kernel(where, received, chain, own, out):
    count = received.shape[0] // 4
    me, core_1 = where[0], where[1] == 1

    def summed(first, number, columns):
        total = received[first, :, columns].astype(F32)
        for i in range(1, number):
            total = total + received[first + i, :, columns].astype(F32)
        return total

    left, right = slice(0, NCOR), slice(NCOR, 2 * NCOR)
    above = jnp.concatenate(
        [summed(4 * jnp.minimum(me + j, count - 1), 4, left) for j in range(1, count)], axis=1
    )
    carry = dot_nt3(above, chain[0], chain[1])
    upper_core = summed(4 * me + 2, 2, left)
    carry = carry + jnp.where(core_1, 0.0, upper_core)
    mine = 4 * me + 2 * where[1]
    both = dot_nt3(carry, own[0], own[1])
    row_0 = (summed(mine, 2, left) + both[:, :NCOR]).astype(BF16)
    row_1 = (summed(mine, 2, right) + both[:, NCOR:]).astype(BF16)
    row_2 = carry.astype(BF16)
    for p in range(out.shape[0]):
        out[p, :, :NCOR] = row_0
        out[p, :, NCOR : 2 * NCOR] = row_1
        out[p, :, 2 * NCOR :] = row_2


def jump_kernel(slot, corner, base_h, base_v, from_right, from_above, corr, jump_h, jump_v):
    def block(a, c, k):
        return corner[a, c, rows(slot, a, c, k), :]

    for a in range(2):
        this = corr[:, a * NCOR : (a + 1) * NCOR]
        twice = jnp.concatenate([this, this], axis=1)
        pair = corr[:, a * NCOR : (a + 2) * NCOR]
        for c in range(2):
            left = from_right[a, :, R:] if c else block(a, 1, 1)
            right = jnp.concatenate([block(a, c, 0), -left], axis=1)
            value = base_h[a, c] - dot(right, twice, 1, 1)
            if c:
                value = value - from_right[a, :, :R].astype(F32)
            jump_h[a, c] = value.astype(BF16)
            down = from_above[c, :, R:] if a else block(1, c, 3)
            right = jnp.concatenate([block(a, c, 2), -down], axis=1)
            value = base_v[a, c] - dot(right, pair, 1, 1)
            if a:
                value = value - from_above[c, :, :R].astype(F32)
            jump_v[a, c] = value.astype(BF16)


def call(kernel, outs, ins, smem=(), flops=0, scratch=()):
    shapes = [jax.ShapeDtypeStruct(shape, dtype) for shape, dtype in outs]
    size = sum(x.size * x.dtype.itemsize for x in list(ins) + shapes)
    result = pl.pallas_call(
        kernel,
        out_shape=shapes,
        in_specs=[
            pl.BlockSpec(memory_space=pltpu.SMEM if i in smem else pltpu.VMEM)
            for i in range(len(ins))
        ],
        out_specs=[pl.BlockSpec(memory_space=pltpu.VMEM)] * len(outs),
        scratch_shapes=list(scratch),
        compiler_params=pltpu.CompilerParams(vmem_limit_bytes=14 * 1024 * 1024),
        cost_estimate=pl.CostEstimate(flops=flops, bytes_accessed=size, transcendentals=0),
    )(*ins)
    return result[0] if len(outs) == 1 else result


def around(value, axes, by):
    count = lax.axis_size(axes)
    return lax.ppermute(value, axes, [(i, (i + by) % count) for i in range(count)])


def along(value, axes, by):
    count = lax.axis_size(axes)
    pairs = [(i, i + by) for i in range(count) if 0 <= i + by < count]
    return lax.ppermute(value, axes, pairs)


def on_device(lam_h, lam_v, panel, corner, diag, link, slot):
    nz, chips, plane = lax.axis_size("z"), lax.axis_size(CHIPS), lax.axis_size(PLANE)
    cols = R // nz
    where = jnp.stack([lax.axis_index(CHIPS), lax.axis_index("core")]).astype(jnp.int32)
    flat_h, flat_v = lam_h.reshape(2, 2 * E, R), lam_v.reshape(2, 2 * E, R)

    left = around(lam_h[:, 1], CIRC, 1)
    below = along(lam_v[1], AXIAL, 1)

    pair = call(pair_kernel, [((NCOR, NCOR), F32)], [link], flops=6 * 2 * NCOR**3)
    other = around(pair, "core", 1)

    part, w1, w3 = call(
        prep_kernel,
        [((R, 2 * NCOR), F32), ((2, E, NCOR), BF16), ((2, E, NCOR), BF16)],
        [slot, panel, corner, flat_h, flat_v],
        smem=(0,),
        flops=2 * (4 * P_SIZE * P_SIZE * NCOR + 10 * E * R * NCOR),
    )
    partial = call(
        halo_kernel,
        [((R, 2 * NCOR), BF16)],
        [part, w1, w3, left, below],
        flops=2 * 4 * E * R * NCOR,
    )
    scattered = lax.all_to_all(partial.reshape(nz, cols, 2 * NCOR), "z", 0, 0)

    chip, terms = call(
        chip_kernel,
        [((chips, NCOR, NCOR), F32), ((2, 3 * NCOR, 2 * NCOR), BF16)],
        [where[1:], diag, link, pair, other],
        smem=(0,),
        flops=6 * 4 * 2 * NCOR**3,
    )
    every_chip = lax.all_to_all(chip, CHIPS, 0, 0)
    chain, own = call(
        chain_kernel,
        [((2, NCOR, (chips - 1) * NCOR), BF16), ((2, 2 * NCOR, NCOR), BF16)],
        [where, other, pair, link, every_chip],
        smem=(0,),
        flops=6 * chips * 2 * NCOR**3,
    )

    base_h, base_v, send_h, send_v = call(
        flex_kernel,
        [((2, 2, E, R), F32)] * 2 + [((2, E, R + NCOR), BF16)] * 2,
        [slot, panel, corner, lam_h, lam_v, left, below],
        smem=(0,),
        flops=4 * 2 * P_SIZE * P_SIZE * R,
        scratch=[pltpu.VMEM((P_SIZE, R), BF16), pltpu.VMEM((P_SIZE, R), F32)],
    )
    from_right = around(send_h, CIRC, -1)
    from_above = along(send_v, AXIAL, -1)

    vectors = call(
        sum_kernel,
        [((plane, cols, 2 * NCOR), BF16)],
        [where, scattered, terms],
        smem=(0,),
        flops=3 * 2 * cols * 6 * NCOR**2,
    )
    gathered = lax.all_to_all(vectors, PLANE, 0, 0)
    mine = call(
        carry_kernel,
        [((nz, cols, 3 * NCOR), BF16)],
        [where, gathered, chain, own],
        smem=(0,),
        flops=3 * 2 * cols * (chips + 2) * NCOR**2,
    )
    corr = lax.all_to_all(mine, "z", 0, 0).reshape(R, 3 * NCOR)
    jump_h, jump_v = call(
        jump_kernel,
        [((2, 2, E, R), BF16)] * 2,
        [slot, corner, base_h, base_v, from_right, from_above, corr],
        smem=(0,),
        flops=2 * 8 * E * R * 2 * NCOR,
    )
    return jump_h, jump_v


def solution(mesh):
    fine = Mesh(mesh.devices.reshape(SPLIT), AXIAL + CIRC)
    return jax.shard_map(
        on_device,
        mesh=fine,
        in_specs=(P(AXIAL, CIRC),) * 4 + (P(AXIAL),) * 2 + (P(AXIAL, CIRC),),
        out_specs=(P(AXIAL, CIRC),) * 2,
        check_vma=False,
    )
```

time: 467 us -> 132 us (0.28)
  the two profiles are of different devices: /device:TPU:6 before, /device:TPU:30 now
where the time goes in v1:
time: 132 us; the launch traced here: 131 us
  starting transfers between devices  53.4 us (40%)
  waiting for transfers between devices  40.9 us (31%)
  local copies, waits for them, and re-layouts  22.2 us (17%)
  Pallas kernels  13.4 us (10%)
    unnamed x56, local copies, waits for them, and re-layouts  20.2 us
    ppermute x3, waiting for transfers between devices, around(): lax.ppermute(value, axes, [(i, (i + by) % count) for i in range(count)])  18.3 us
    all_to_all x1, starting transfers between devices, on_device(): scattered = lax.all_to_all(partial.reshape(nz, cols, 2 * NCOR), 'z', 0, 0)  14.4 us
    pallas_call x9, Pallas kernels, call(): pl.pallas_call(kernel, out_shape=shapes, in_specs=[pl.BlockSpec(memory_sp...  13.4 us
    all_to_all x1, waiting for transfers between devices, on_device(): scattered = lax.all_to_all(partial.reshape(nz, cols, 2 * NCOR), 'z', 0, 0)  13.2 us
    ppermute x3, starting transfers between devices, around(): lax.ppermute(value, axes, [(i, (i + by) % count) for i in range(count)])  10.8 us
    all_to_all x1, starting transfers between devices, on_device(): gathered = lax.all_to_all(vectors, PLANE, 0, 0)  8.94 us
    all_to_all x1, starting transfers between devices, on_device(): every_chip = lax.all_to_all(chip, CHIPS, 0, 0)  8.02 us
  transfers between devices with their start and end apart: 9, of which 5 were waited for; matrix products, arithmetic and copies ran while one was open for 1% of the time, Pallas kernels for 6%

profile of v1, /device:TPU:30, one launch (start us, length us, event | category | flops | bytes accessed | tf_op | source)
XLA Modules:
  0.0 130.8 jit_solution(11356119242933055371)
XLA Ops:
  1.6 1.9 %collective-permute-start.1 = (bf16[2,128,512]{2,1,0:T(8,128)(2,1)S(1)}, bf16[2,128,512]{2,1,0:T(8,128)(2,1)S(1)}, u32[]{:S(2)}, u32[]{:S(2)}) collective-permute-start(bf16[2,128,512]{2,1,0:T(8,128)(2,1)S(1)} %slice_bitcast_fusion), channel_id=1, source_target_pairs={{0,32},{32,64},{64,96},{96,128},{128,160},{160,192},{192,224},{224... | collective-permute-start | bytes 786440 | tf_op jit(solution)/shard_map/ppermute | solution.py:240
  3.5 1.0 slice_bitcast_fusion.1
  4.5 4.5 %collective-permute-start = (bf16[2,128,512]{2,1,0:T(8,128)(2,1)S(1)}, bf16[2,128,512]{2,1,0:T(8,128)(2,1)S(1)}, u32[]{:S(2)}, u32[]{:S(2)}) collective-permute-start(bf16[2,128,512]{2,1,0:T(8,128)(2,1)S(1)} %slice_bitcast_fusion.1), channel_id=1, source_target_pairs={{0,1},{1,2},{2,3},{3,4},{4,5},{5,6},{6,7},{7,8},{8,9},{9,10},{10,1... | collective-permute-start | bytes 786440 | tf_op jit(solution)/shard_map/ppermute | solution.py:234
  9.0 1.6 %copy-done = bf16[2,2,512,512]{3,2,1,0:T(8,128)(2,1)S(1)} copy-done((bf16[2,2,512,512]{3,2,1,0:T(8,128)(2,1)S(1)}, bf16[2,2,512,512]{3,2,1,0:T(8,128)(2,1)}, u32[]{:S(2)}) %copy-start) | copy-done | bytes 2097176
  10.6 1.0 copy-done.2
  11.7 1.0 copy-done.4
  12.7 1.0 copy-done.6
  14.4 1.6 %shard_map.87 = (f32[512,256]{1,0:T(8,128)S(1)}, bf16[2,128,128]{2,1,0:T(8,128)(2,1)S(1)}, bf16[2,128,128]{2,1,0:T(8,128)(2,1)S(1)}) custom-call(s32[2,2,4]{2,1,0:T(2,128)S(1)} %copy-done.26, bf16[2,2,512,512]{3,2,1,0:T(8,128)(2,1)S(1)} %copy-done, bf16[2,2,512,128]{3,2,1,0:T(8,128)(2,1)S(1)} %copy-done.2, bf16[2,256,512]{2,1,0:T(8,128)(2,1)S(1)} %bitcast.12, ...), custom_call_target="tpu_custom_call" | custom-call | flops 436207616 | bytes 4325440 | tf_op jit(solution)/shard_map/pallas_call | solution.py:217
  16.1 1.1 shard_map.88
  17.9 14.4 %all-to-all-start = ((bf16[16,32,256]{2,1,0:T(8,128)(2,1)}), bf16[16,32,256]{2,1,0:T(8,128)(2,1)S(1)}, u32[]{:S(2)}, u32[]{:S(2)}) async-start(bf16[16,32,256]{2,1,0:T(8,128)(2,1)} %bitcast.6), calls=%async_computation | async-start | bytes 524288 | tf_op jit(solution)/shard_map/all_to_all | solution.py:268
  32.5 1.9 %collective-permute-start.4 = (f32[128,128]{1,0:T(8,128)S(1)}, f32[128,128]{1,0:T(8,128)S(1)}, u32[]{:S(2)}, u32[]{:S(2)}) collective-permute-start(f32[128,128]{1,0:T(8,128)S(1)} %shard_map.89.pair), channel_id=1, source_target_pairs={{0,32},{32,0},{1,33},{33,1},{2,34},{34,2},{3,35},{35,3},{4,36},{36... | collective-permute-start | bytes 196616 | tf_op jit(solution)/shard_map/ppermute | solution.py:234
  34.5 1.2 collective-permute-done.4.other
  35.7 1.1 shard_map.90
  36.8 13.2 %all-to-all-done.received = bf16[16,32,256]{2,1,0:T(8,128)(2,1)S(1)} async-done(((bf16[16,32,256]{2,1,0:T(8,128)(2,1)}), bf16[16,32,256]{2,1,0:T(8,128)(2,1)S(1)}, u32[]{:S(2)}, u32[]{:S(2)}) %all-to-all-start) | async-done | bytes 262176 | tf_op jit(solution)/shard_map/all_to_all | solution.py:268
  49.9 8.0 %all-to-all-start.2 = ((f32[8,128,128]{2,1,0:T(8,128)}), f32[8,128,128]{2,1,0:T(8,128)}, u32[]{:S(2)}, u32[]{:S(2)}) async-start(f32[8,128,128]{2,1,0:T(8,128)} %get-tuple-element.21), calls=%async_computation.2 | async-start | bytes 1048576 | tf_op jit(solution)/shard_map/all_to_all | solution.py:277
  59.7 4.3 %all-to-all-done.2.chips = f32[8,128,128]{2,1,0:T(8,128)} async-done(((f32[8,128,128]{2,1,0:T(8,128)}), f32[8,128,128]{2,1,0:T(8,128)}, u32[]{:S(2)}, u32[]{:S(2)}) %all-to-all-start.2) | async-done | bytes 524320 | tf_op jit(solution)/shard_map/all_to_all | solution.py:277
  64.1 8.9 %all-to-all-start.1 = ((bf16[32,32,256]{2,1,0:T(8,128)(2,1)}), bf16[32,32,256]{2,1,0:T(8,128)(2,1)}, u32[]{:S(2)}, u32[]{:S(2)}) async-start(bf16[32,32,256]{2,1,0:T(8,128)(2,1)} %copy-done.8), calls=%async_computation.1 | async-start | bytes 1048576 | tf_op jit(solution)/shard_map/all_to_all | solution.py:304
  73.0 2.4 %shard_map.92 = (bf16[2,128,896]{2,1,0:T(8,128)(2,1)S(1)}, bf16[2,256,128]{2,1,0:T(8,128)(2,1)S(1)}) custom-call(s32[2]{0:T(128)S(1)} %pad_add_fusion.where, f32[128,128]{1,0:T(8,128)S(1)} %collective-permute-done.4.other, f32[128,128]{1,0:T(8,128)S(1)} %shard_map.89.pair, f32[2,128,128]{2,1,0:T(8,128)S(1)} %copy-done.10, f32[8,128,128]{2,1,0:T(8,128)} %all-to-all-done.2.chips), custom_call_target="tpu_custom_call" | custom-call | flops 201326592 | bytes 1376264 | tf_op jit(solution)/shard_map/pallas_call | solution.py:217
  76.2 5.0 %all-to-all-done.1.received = bf16[32,32,256]{2,1,0:T(8,128)(2,1)} async-done(((bf16[32,32,256]{2,1,0:T(8,128)(2,1)}), bf16[32,32,256]{2,1,0:T(8,128)(2,1)}, u32[]{:S(2)}, u32[]{:S(2)}) %all-to-all-start.1) | async-done | bytes 524320 | tf_op jit(solution)/shard_map/all_to_all | solution.py:304
  81.2 1.0 copy-done.20
  82.2 1.7 %shard_map.93 = bf16[16,32,384]{2,1,0:T(8,128)(2,1)S(1)} custom-call(s32[2]{0:T(128)S(1)} %pad_add_fusion.where, bf16[32,32,256]{2,1,0:T(8,128)(2,1)} %all-to-all-done.1.received, bf16[2,128,896]{2,1,0:T(8,128)(2,1)S(1)} %copy-done.20, bf16[2,256,128]{2,1,0:T(8,128)(2,1)S(1)} %get-tuple-element.23.own), custom_call_target="tpu_custom_call" | custom-call | flops 31457280 | bytes 1507336 | tf_op jit(solution)/shard_map/pallas_call | solution.py:217
  84.6 7.4 %all-to-all-start.3 = ((bf16[16,32,384]{2,1,0:T(8,128)(2,1)}), bf16[16,32,384]{2,1,0:T(8,128)(2,1)S(1)}, u32[]{:S(2)}, u32[]{:S(2)}) async-start(bf16[16,32,384]{2,1,0:T(8,128)(2,1)} %copy-done.9), calls=%async_computation.3 | async-start | bytes 786432 | tf_op jit(solution)/shard_map/all_to_all | solution.py:312
  92.1 1.0 copy-done.7
  95.0 2.2 %shard_map.86 = (f32[2,2,128,512]{3,2,1,0:T(8,128)S(1)}, f32[2,2,128,512]{3,2,1,0:T(8,128)S(1)}, bf16[2,128,640]{2,1,0:T(8,128)(2,1)S(1)}, bf16[2,128,640]{2,1,0:T(8,128)(2,1)S(1)}) custom-call(s32[2,2,4]{2,1,0:T(2,128)S(1)} %copy-done.27, bf16[2,2,512,512]{3,2,1,0:T(8,128)(2,1)S(1)} %copy-done.1, bf16[2,2,512,128]{3,2,1,0:T(8,128)(2,1)S(1)} %copy-done.3, ...), custom_call_target="tpu_custom_call" | custom-call | flops 1073741824 | bytes 6946880 | tf_op jit(solution)/shard_map/pallas_call | solution.py:217
  97.3 1.0 copy-done.11
  98.2 1.0 copy-done.13
  99.2 4.3 %collective-permute-start.2 = (bf16[2,128,640]{2,1,0:T(8,128)(2,1)S(1)}, bf16[2,128,640]{2,1,0:T(8,128)(2,1)S(1)}, u32[]{:S(2)}, u32[]{:S(2)}) collective-permute-start(bf16[2,128,640]{2,1,0:T(8,128)(2,1)S(1)} %get-tuple-element.15), channel_id=1, source_target_pairs={{0,31},{1,0},{2,1},{3,2},{4,3},{5,4},{6,5},{7,6},{8,7},{9,8},{10,9... | collective-permute-start | bytes 983048 | tf_op jit(solution)/shard_map/ppermute | solution.py:234
  103.6 1.9 %collective-permute-start.3 = (bf16[2,128,640]{2,1,0:T(8,128)(2,1)S(1)}, bf16[2,128,640]{2,1,0:T(8,128)(2,1)S(1)}, u32[]{:S(2)}, u32[]{:S(2)}) collective-permute-start(bf16[2,128,640]{2,1,0:T(8,128)(2,1)S(1)} %get-tuple-element.16), channel_id=1, source_target_pairs={{32,0},{64,32},{96,64},{128,96},{160,128},{192,160},{224,192},{256... | collective-permute-start | bytes 983048 | tf_op jit(solution)/shard_map/ppermute | solution.py:240
  105.5 17.1 %collective-permute-done.2.from_right = bf16[2,128,640]{2,1,0:T(8,128)(2,1)S(1)} collective-permute-done((bf16[2,128,640]{2,1,0:T(8,128)(2,1)S(1)}, bf16[2,128,640]{2,1,0:T(8,128)(2,1)S(1)}, u32[]{:S(2)}, u32[]{:S(2)}) %collective-permute-start.2) | collective-permute-done | bytes 327712 | tf_op jit(solution)/shard_map/ppermute | solution.py:234
  124.1 1.2 copy-done.12
  125.3 1.2 copy-done.14
  128.5 2.3 %shard_map.94 = (bf16[2,2,128,512]{3,2,1,0:T(8,128)(2,1)}, bf16[2,2,128,512]{3,2,1,0:T(8,128)(2,1)}) custom-call(s32[2,2,4]{2,1,0:T(2,128)S(1)} %copy-done.27, bf16[2,2,512,128]{3,2,1,0:T(8,128)(2,1)S(1)} %copy-done.3, f32[2,2,128,512]{3,2,1,0:T(8,128)S(1)} %copy-done.12, f32[2,2,128,512]{3,2,1,0:T(8,128)S(1)} %copy-done.14, ...), custom_call_target="tpu_custom_call" | custom-call | flops 268435456 | bytes 4718656 | tf_op jit(solution)/shard_map/pallas_call | solution.py:217
  (54 shorter events, 11.2 us)
Async XLA Ops:
  1.6 14.4 %collective-permute-start.1 = (bf16[2,128,512]{2,1,0:T(8,128)(2,1)S(1)}, bf16[2,128,512]{2,1,0:T(8,128)(2,1)S(1)}, u32[]{:S(2)}, u32[]{:S(2)}) collective-permute-start(bf16[2,128,512]{2,1,0:T(8,128)(2,1)S(1)} %slice_bitcast_fusion), channel_id=1, source_target_pairs={{0,32},{32,64},{64,96},{96,128},{128,160},{160,192},{192,224},{224... | collective-permute-start | bytes 786440 | tf_op jit(solution)/shard_map/ppermute | solution.py:240
  4.5 11.5 %collective-permute-start = (bf16[2,128,512]{2,1,0:T(8,128)(2,1)S(1)}, bf16[2,128,512]{2,1,0:T(8,128)(2,1)S(1)}, u32[]{:S(2)}, u32[]{:S(2)}) collective-permute-start(bf16[2,128,512]{2,1,0:T(8,128)(2,1)S(1)} %slice_bitcast_fusion.1), channel_id=1, source_target_pairs={{0,1},{1,2},{2,3},{3,4},{4,5},{5,6},{6,7},{7,8},{8,9},{9,10},{10,1... | collective-permute-start | bytes 786440 | tf_op jit(solution)/shard_map/ppermute | solution.py:234
  9.0 1.6 %copy-start = (bf16[2,2,512,512]{3,2,1,0:T(8,128)(2,1)S(1)}, bf16[2,2,512,512]{3,2,1,0:T(8,128)(2,1)}, u32[]{:S(2)}) copy-start(bf16[2,2,512,512]{3,2,1,0:T(8,128)(2,1)} %panel.3) | copy-start | bytes 6291460
  10.6 1.0 copy-start.2
  11.7 1.0 copy-start.4
  12.7 1.0 copy-start.6
  14.4 17.9 %copy-start.10 = (f32[2,128,128]{2,1,0:T(8,128)S(1)}, f32[2,128,128]{2,1,0:T(8,128)}, u32[]{:S(2)}) copy-start(f32[2,128,128]{2,1,0:T(8,128)} %link.5) | copy-start | bytes 393220
  14.4 21.3 %copy-start.25 = (f32[2,128,128]{2,1,0:T(8,128)S(1)}, f32[2,128,128]{2,1,0:T(8,128)}, u32[]{:S(2)}) copy-start(f32[2,128,128]{2,1,0:T(8,128)} %diag.1) | copy-start | bytes 393220
  16.1 1.1 copy-start.17
  17.9 32.1 %all-to-all-start = ((bf16[16,32,256]{2,1,0:T(8,128)(2,1)}), bf16[16,32,256]{2,1,0:T(8,128)(2,1)S(1)}, u32[]{:S(2)}, u32[]{:S(2)}) async-start(bf16[16,32,256]{2,1,0:T(8,128)(2,1)} %bitcast.6), calls=%async_computation | async-start | bytes 524288 | tf_op jit(solution)/shard_map/all_to_all | solution.py:268
  32.5 3.1 %collective-permute-start.4 = (f32[128,128]{1,0:T(8,128)S(1)}, f32[128,128]{1,0:T(8,128)S(1)}, u32[]{:S(2)}, u32[]{:S(2)}) collective-permute-start(f32[128,128]{1,0:T(8,128)S(1)} %shard_map.89.pair), channel_id=1, source_target_pairs={{0,32},{32,0},{1,33},{33,1},{2,34},{34,2},{3,35},{35,3},{4,36},{36... | collective-permute-start | bytes 196616 | tf_op jit(solution)/shard_map/ppermute | solution.py:234
  49.9 14.1 %all-to-all-start.2 = ((f32[8,128,128]{2,1,0:T(8,128)}), f32[8,128,128]{2,1,0:T(8,128)}, u32[]{:S(2)}, u32[]{:S(2)}) async-start(f32[8,128,128]{2,1,0:T(8,128)} %get-tuple-element.21), calls=%async_computation.2 | async-start | bytes 1048576 | tf_op jit(solution)/shard_map/all_to_all | solution.py:277
  58.0 34.0 %copy-start.27 = (s32[2,2,4]{2,1,0:T(2,128)S(1)}, s32[2,2,4]{2,1,0:T(2,128)}, u32[]{:S(2)}) copy-start(s32[2,2,4]{2,1,0:T(2,128)} %slot.5) | copy-start | bytes 196
  58.9 0.8 copy-start.8
  59.7 32.3 %copy-start.1 = (bf16[2,2,512,512]{3,2,1,0:T(8,128)(2,1)S(1)}, bf16[2,2,512,512]{3,2,1,0:T(8,128)(2,1)}, u32[]{:S(2)}) copy-start(bf16[2,2,512,512]{3,2,1,0:T(8,128)(2,1)} %panel.3) | copy-start | bytes 6291460
  59.7 32.3 %copy-start.3 = (bf16[2,2,512,128]{3,2,1,0:T(8,128)(2,1)S(1)}, bf16[2,2,512,128]{3,2,1,0:T(8,128)(2,1)}, u32[]{:S(2)}) copy-start(bf16[2,2,512,128]{3,2,1,0:T(8,128)(2,1)} %corner.5) | copy-start | bytes 1572868
  59.7 32.3 %copy-start.5 = (bf16[2,2,128,512]{3,2,1,0:T(8,128)(2,1)S(1)}, bf16[2,2,128,512]{3,2,1,0:T(8,128)(2,1)}, u32[]{:S(2)}) copy-start(bf16[2,2,128,512]{3,2,1,0:T(8,128)(2,1)} %lam_h.1) | copy-start | bytes 1572868
  64.1 17.1 %all-to-all-start.1 = ((bf16[32,32,256]{2,1,0:T(8,128)(2,1)}), bf16[32,32,256]{2,1,0:T(8,128)(2,1)}, u32[]{:S(2)}, u32[]{:S(2)}) async-start(bf16[32,32,256]{2,1,0:T(8,128)(2,1)} %copy-done.8), calls=%async_computation.1 | async-start | bytes 1048576 | tf_op jit(solution)/shard_map/all_to_all | solution.py:304
  75.4 0.8 copy-start.19
  81.2 1.0 copy-start.20
  84.6 39.5 %all-to-all-start.3 = ((bf16[16,32,384]{2,1,0:T(8,128)(2,1)}), bf16[16,32,384]{2,1,0:T(8,128)(2,1)S(1)}, u32[]{:S(2)}, u32[]{:S(2)}) async-start(bf16[16,32,384]{2,1,0:T(8,128)(2,1)} %copy-done.9), calls=%async_computation.3 | async-start | bytes 786432 | tf_op jit(solution)/shard_map/all_to_all | solution.py:312
  92.1 1.0 copy-start.7
  93.1 0.9 copy-start.16
  94.1 0.9 copy-start.18
  97.3 1.0 copy-start.11
  98.2 1.0 copy-start.13
  99.2 23.4 %collective-permute-start.2 = (bf16[2,128,640]{2,1,0:T(8,128)(2,1)S(1)}, bf16[2,128,640]{2,1,0:T(8,128)(2,1)S(1)}, u32[]{:S(2)}, u32[]{:S(2)}) collective-permute-start(bf16[2,128,640]{2,1,0:T(8,128)(2,1)S(1)} %get-tuple-element.15), channel_id=1, source_target_pairs={{0,31},{1,0},{2,1},{3,2},{4,3},{5,4},{6,5},{7,6},{8,7},{9,8},{10,9... | collective-permute-start | bytes 983048 | tf_op jit(solution)/shard_map/ppermute | solution.py:234
  103.6 19.8 %collective-permute-start.3 = (bf16[2,128,640]{2,1,0:T(8,128)(2,1)S(1)}, bf16[2,128,640]{2,1,0:T(8,128)(2,1)S(1)}, u32[]{:S(2)}, u32[]{:S(2)}) collective-permute-start(bf16[2,128,640]{2,1,0:T(8,128)(2,1)S(1)} %get-tuple-element.16), channel_id=1, source_target_pairs={{32,0},{64,32},{96,64},{128,96},{160,128},{192,160},{224,192},{256... | collective-permute-start | bytes 983048 | tf_op jit(solution)/shard_map/ppermute | solution.py:240
  124.1 1.2 copy-start.12
  125.3 1.2 copy-start.14
  126.6 1.0 copy-start.22
  127.5 1.0 copy-start.24
  (5 other events, 3.6 us)
